TPU v7x, 32 devices: a whole 2x2x4 slice. The times are simulated.
32 devices in a mesh: groups: 2 (over x), lon: 16 (over z, y, core).
Axes of the slice: x: 2, y: 2, z: 4, core: 2. Of those that a mesh axis runs over, the one named last changes fastest.
Arguments:
- mesh_latent: bfloat16 [3072, 512], P(('groups', 'lon')), parts along dimension 0, may hold values from -6 to 6
- mesh_edges: bfloat16 [36864, 512], P(('groups', 'lon')), parts along dimension 0, may hold values from -6 to 6
- proc_slot: int32 [36864], P(('groups', 'lon')), parts along dimension 0, may hold values from 0 to 127, as said below
- proc_receiver: int32 [36864], P(('groups', 'lon')), parts along dimension 0, may hold values from 0 to 96, as said below
- proc_lists: int32 [512, 8], P(('groups', 'lon')), parts along dimension 0, may hold values from 0 to 95
- grid_latent: bfloat16 [16384, 512], P(('groups', 'lon')), parts along dimension 0, may hold values from -6 to 6
- grid_edges: bfloat16 [49152, 512], P(('groups', 'lon')), parts along dimension 0, may hold values from -6 to 6
- grid_sender: int32 [49152], P(('groups', 'lon')), parts along dimension 0, may hold values from 0 to 1535, as said below
- proc_edge_in: bfloat16 [1536, 512], replicated, may hold values from -0.15625 to 0.15625
- proc_edge_out: bfloat16 [512, 512], replicated, may hold values from -0.25 to 0.25
- proc_node_in: bfloat16 [1024, 512], replicated, may hold values from -0.1875 to 0.1875
- proc_node_out: bfloat16 [512, 512], replicated, may hold values from -0.25 to 0.25
- grid_edge_in: bfloat16 [1536, 512], replicated, may hold values from -0.15625 to 0.15625
- grid_edge_out: bfloat16 [512, 512], replicated, may hold values from -0.25 to 0.25
- grid_node_in: bfloat16 [1024, 512], replicated, may hold values from -0.1875 to 0.1875
- grid_node_out: bfloat16 [512, 512], replicated, may hold values from -0.25 to 0.25
- proc_edge_gain: float32 [512], replicated, may hold values from 0.25 to 1.75
- proc_node_gain: float32 [512], replicated, may hold values from 0.25 to 1.75
- grid_edge_gain: float32 [512], replicated, may hold values from 0.25 to 1.75
- grid_node_gain: float32 [512], replicated, may hold values from 0.25 to 1.75
Outputs:
- mesh_new: bfloat16 [3072, 512], P(('groups', 'lon')), parts along dimension 0
- grid_new: bfloat16 [16384, 512], P(('groups', 'lon')), parts along dimension 0
There are 2 independent parts, one for each index of `groups`. A program takes and returns all parts, laid end to end along the dimension named above; an argument that names none is the same for every part. Nothing has to cross between parts.
Inputs may be any that keep to these rules, and one draw needn't show every extreme that they name: `proc_lists`: every list holds exactly 8 entries; entries may repeat. `proc_slot`: slot s of an edge of device r names column s % 8 of device r's list for owner s // 8. `proc_receiver`: 96 marks an empty slot; on some device no slot is empty. `grid_sender`: the sender of a decoder edge into a grid node of device r is a mesh node of device r - 1, r or r + 1 (modulo 16).
All inputs are finite; a program needn't handle non-finite values.
Results may differ from a plain program's by a relative error of at most 0.011.
Values may be sent and summed in bfloat16 or wider, within the bound.
A program may use at most 128 MiB of HBM per device.

v0:
```python
import jax
import jax.numpy as jnp
from jax import lax
from jax.sharding import PartitionSpec as P

NEAR = 3


EPSILON = 1e-05


def padded(block, sides, width):
    for axis, dim in sides:
        count = lax.axis_size(axis)
        forward = [(i, i + 1) for i in range(count - 1)]
        forward.append((count - 1, 0))
        backward = [(target, source) for source, target in forward]
        low = lax.ppermute(
            lax.slice_in_dim(block, block.shape[dim] - width, None, axis=dim), axis, forward
        )
        high = lax.ppermute(lax.slice_in_dim(block, 0, width, axis=dim), axis, backward)
        block = jnp.concatenate([low, block, high], axis=dim)
    return block


def layer_norm(values, gain):
    center = values - jnp.mean(values, axis=-1, keepdims=True)
    spread = jnp.mean(center * center, axis=-1, keepdims=True)
    return center * lax.rsqrt(spread + EPSILON) * gain


def second_layer(first_sum, w_second, gain):
    hidden = jax.nn.silu(first_sum).astype(jnp.bfloat16)
    return layer_norm(jnp.dot(hidden, w_second, preferred_element_type=jnp.float32), gain)


def local(
    mesh_latent,
    mesh_edges,
    proc_slot,
    proc_receiver,
    proc_lists,
    grid_latent,
    grid_edges,
    grid_sender,
    proc_edge_in,
    proc_edge_out,
    proc_node_in,
    proc_node_out,
    grid_edge_in,
    grid_edge_out,
    grid_node_in,
    grid_node_out,
    proc_edge_gain,
    proc_node_gain,
    grid_edge_gain,
    grid_node_gain,
):
    rows_mesh = mesh_latent.shape[0]
    width = mesh_latent.shape[1]
    devices = lax.axis_size("lon")
    cap_rows = proc_lists.shape[1]
    owner_dev = proc_slot // cap_rows
    list_col = proc_slot % cap_rows
    sender_id = owner_dev * rows_mesh + proc_lists[owner_dev, list_col]
    gathered = lax.all_gather(mesh_latent, "lon", axis=0, tiled=True)
    senders = jnp.take(gathered, sender_id, axis=0)
    receiver_term = jnp.dot(
        mesh_latent, proc_edge_in[2 * width :], preferred_element_type=jnp.float32
    )
    clipped = jnp.minimum(proc_receiver, rows_mesh - 1)
    edge_sum = jnp.dot(mesh_edges, proc_edge_in[:width], preferred_element_type=jnp.float32)
    edge_sum = edge_sum + jnp.take(receiver_term, clipped, axis=0)
    edge_sum = edge_sum + jnp.dot(
        senders, proc_edge_in[width : 2 * width], preferred_element_type=jnp.float32
    )
    message = second_layer(edge_sum, proc_edge_out, proc_edge_gain).astype(jnp.bfloat16)
    one_hot = (jnp.arange(rows_mesh, dtype=jnp.int32)[:, None] == proc_receiver[None, :]).astype(
        jnp.bfloat16
    )
    incoming = jnp.dot(one_hot, message, preferred_element_type=jnp.float32).astype(jnp.bfloat16)
    node_sum = jnp.dot(mesh_latent, proc_node_in[:width], preferred_element_type=jnp.float32)
    node_sum = node_sum + jnp.dot(
        incoming, proc_node_in[width:], preferred_element_type=jnp.float32
    )
    mesh_new = (
        mesh_latent.astype(jnp.float32) + second_layer(node_sum, proc_node_out, proc_node_gain)
    ).astype(jnp.bfloat16)
    window = padded(mesh_new, (("lon", 0),), rows_mesh)
    here = lax.axis_index("lon")
    sender_dev = grid_sender // rows_mesh
    place = (sender_dev - here + 1) % devices * rows_mesh + grid_sender % rows_mesh
    grid_senders = jnp.take(window, place, axis=0)
    grid_receiver_term = jnp.dot(
        grid_latent, grid_edge_in[2 * width :], preferred_element_type=jnp.float32
    )
    grid_sum = jnp.dot(grid_edges, grid_edge_in[:width], preferred_element_type=jnp.float32)
    grid_sum = grid_sum + jnp.repeat(grid_receiver_term, NEAR, axis=0)
    grid_sum = grid_sum + jnp.dot(
        grid_senders, grid_edge_in[width : 2 * width], preferred_element_type=jnp.float32
    )
    grid_message = second_layer(grid_sum, grid_edge_out, grid_edge_gain).astype(jnp.bfloat16)
    grid_incoming = jnp.sum(
        grid_message.astype(jnp.float32).reshape(grid_latent.shape[0], NEAR, width), axis=1
    ).astype(jnp.bfloat16)
    grid_node_sum = jnp.dot(grid_latent, grid_node_in[:width], preferred_element_type=jnp.float32)
    grid_node_sum = grid_node_sum + jnp.dot(
        grid_incoming, grid_node_in[width:], preferred_element_type=jnp.float32
    )
    grid_new = (
        grid_latent.astype(jnp.float32) + second_layer(grid_node_sum, grid_node_out, grid_node_gain)
    ).astype(jnp.bfloat16)
    return (mesh_new, grid_new)


def solution(mesh):
    placed = (
        P(("groups", "lon"), None),
        P(("groups", "lon"), None),
        P(("groups", "lon")),
        P(("groups", "lon")),
        P(("groups", "lon"), None),
        P(("groups", "lon"), None),
        P(("groups", "lon"), None),
        P(("groups", "lon")),
        P(),
        P(),
        P(),
        P(),
        P(),
        P(),
        P(),
        P(),
        P(),
        P(),
        P(),
        P(),
    )
    return jax.shard_map(
        local,
        mesh=mesh,
        in_specs=placed,
        out_specs=(P(("groups", "lon"), None), P(("groups", "lon"), None)),
        check_vma=False,
    )
```

profile of v0, /device:TPU:0, one launch (start us, length us, event | category | flops | bytes accessed | tf_op | source)
XLA Modules:
  0.0 111.8 jit_solution(9695154024455799821)
XLA Ops:
  7.9 1.6 %fusion.23 = f32[512,512]{1,0:T(8,128)S(1)} fusion(bf16[512,512]{1,0:T(8,128)(2,1)} %param.25, bf16[1536,512]{1,0:T(8,128)(2,1)} %param.32), kind=kOutput, calls=%fused_computation.34 | convolution fusion | flops 268435456 | bytes 2097152 | tf_op jit(solution)/shard_map/dot_general | solution.py:94
  10.6 2.7 %broadcast_in_dim.67 = f32[512,3,512]{2,1,0:T(4,128)} broadcast(f32[512,512]{1,0:T(8,128)S(1)} %fusion.23), dimensions={0,2} | broadcast | bytes 4194304 | tf_op jit(solution)/shard_map/broadcast_in_dim | solution.py:98
  13.3 6.0 %reshape.81 = f32[1536,512]{1,0:T(8,128)} reshape(f32[512,3,512]{2,1,0:T(4,128)} %broadcast_in_dim.67) | data formatting | bytes 6291456 | tf_op jit(solution)/shard_map/reshape | solution.py:98
  19.3 4.9 %gather_fusion.1 = s32[1152]{0:T(1024)S(1)} fusion(s32[16,8]{0,1:T(8,128)S(1)} %copy-done.1, s32[1152]{0:T(1024)S(1)} %fusion.47), kind=kCustom, calls=%fused_computation.1 | custom fusion | bytes 18432 | tf_op jit(solution)/shard_map/gather | solution.py:65
  24.3 1.3 %fusion.31 = f32[96,512]{1,0:T(8,128)S(1)} fusion(bf16[96,512]{1,0:T(8,128)(2,1)S(1)} %copy-done.7, bf16[1536,512]{1,0:T(8,128)(2,1)} %param.28), kind=kOutput, calls=%fused_computation.41 | convolution fusion | flops 50331648 | bytes 819200 | tf_op jit(solution)/shard_map/dot_general | solution.py:68
  25.6 4.3 %gather_fusion = f32[1152,512]{1,0:T(8,128)} fusion(f32[96,512]{1,0:T(8,128)S(1)} %fusion.31, s32[2048]{0:T(1024)S(1)} %pad_clamp_fusion.2), kind=kCustom, calls=%fused_computation | custom fusion | bytes 4723200 | tf_op jit(solution)/shard_map/jit(_take)/gather | solution.py:73
  31.6 2.4 %fusion.26 = f32[512,512]{1,0:T(8,128)} fusion(bf16[512,512]{1,0:T(8,128)(2,1)S(1)} %copy-done.5, bf16[1024,512]{1,0:T(8,128)(2,1)} %param.34), kind=kOutput, calls=%fused_computation.37 | convolution fusion | flops 268435456 | bytes 2097152 | tf_op jit(solution)/shard_map/dot_general | solution.py:106
  34.0 3.8 %convolution_add_fusion.1 = f32[1152,512]{1,0:T(8,128)} fusion(bf16[1152,512]{1,0:T(8,128)(2,1)} %param.21, f32[1152,512]{1,0:T(8,128)S(1)} %copy-done.4, pred[1152]{0:T(1024)(128)(4,1)S(1)} %compare_and_fusion.2, bf16[1536,512]{1,0:T(8,128)(2,1)} %param.28), kind=kOutput, calls=%fused_computation.5 | convolution fusion | flops 605159424 | bytes 6423680 | tf_op jit(solution)/shard_map/dot_general | solution.py:72
  37.8 3.8 %convolution_add_fusion.3 = f32[1536,512]{1,0:T(8,128)} fusion(f32[1536,512]{1,0:T(8,128)S(1)} %copy-done.2, bf16[1536,512]{1,0:T(8,128)(2,1)S(1)} %copy-done, bf16[1536,512]{1,0:T(8,128)(2,1)} %param.32), kind=kOutput, calls=%fused_computation.7 | convolution fusion | flops 806092800 | bytes 8388608 | tf_op jit(solution)/shard_map/dot_general | solution.py:97
  41.5 11.2 %all-gather.2.cloned.1.call-done = bf16[1536,512]{1,0:T(8,128)(2,1)} async-done(((bf16[96,512]{1,0:T(8,128)(2,1)}), bf16[1536,512]{1,0:T(8,128)(2,1)}) %all-gather.2.cloned.1.call-update) | async-done | bytes 1572880 | tf_op jit(solution)/shard_map/all_gather | solution.py:66
  52.7 6.3 %gather_fusion.2 = bf16[1152,512]{1,0:T(8,128)(2,1)} fusion(bf16[1536,512]{1,0:T(8,128)(2,1)} %all-gather.2.cloned.1.call-done, s32[2048]{0:T(1024)S(1)} %pad_clamp_fusion.1), kind=kCustom, calls=%fused_computation.2 | custom fusion | bytes 2363904 | tf_op jit(solution)/shard_map/jit(_take)/gather | solution.py:67
  59.1 5.3 %fusion.60 = (f32[1152]{0:T(1024)S(1)}, f32[1152,512]{0,1:T(8,128)}) fusion(bf16[512,512]{1,0:T(8,128)(2,1)S(1)} %copy-done.18, f32[1152,512]{1,0:T(8,128)} %convolution_add_fusion.1, bf16[1152,512]{1,0:T(8,128)(2,1)} %gather_fusion.2, pred[1152]{0:T(1024)(128)(4,1)S(1)} %get-tuple-element.8, bf16[1536,512]{1,0:T(8,128)(2,1)} %param.28), kind=kOutput, calls=%fused_computation.101 | convolution fusion | flops 1212676992 | bytes 6952576 | tf_op jit(solution)/shard_map/dot_general | solution.py:34
  64.4 2.0 %multiply_reduce_fusion.1 = f32[1152]{0:T(1024)S(1)} fusion(f32[1152,512]{0,1:T(8,128)} %get-tuple-element.11, f32[1152]{0:T(1024)S(1)} %broadcast_multiply_fusion.1), kind=kLoop, calls=%fused_computation.12 | loop fusion | flops 1768320 | bytes 2368512 | tf_op jit(solution)/shard_map/reduce_sum | solution.py:28
  67.0 2.4 %multiply_convert_fusion.10 = bf16[96,512]{1,0:T(8,128)(2,1)S(1)} fusion(f32[96,512]{1,0:T(8,128)S(1)} %copy-done.11, bf16[1024,512]{1,0:T(8,128)(2,1)S(1)} %copy-done.10, f32[1152,512]{0,1:T(8,128)} %get-tuple-element.11, f32[512]{0:T(512)} %param.36, f32[1152]{0:T(1024)} %add_rsqrt_fusion.1, f32[1152]{0:T(1024)S(1)} %broadcast_multiply_fusion.1, ...), kind=kOutput, calls=%fused_computation.51 | convolution fusion | flops 166391808 | bytes 3201536 | tf_op jit(solution)/shard_map/dot_general | solution.py:83
  71.1 4.2 %collective-permute-start.1 = (bf16[96,512]{1,0:T(8,128)(2,1)S(1)}, bf16[96,512]{1,0:T(8,128)(2,1)S(1)}, u32[]{:S(2)}, u32[]{:S(2)}) collective-permute-start(bf16[96,512]{1,0:T(8,128)(2,1)S(1)} %add_convert_fusion.1), channel_id=1, source_target_pairs={{1,0},{2,1},{3,2},{4,3},{5,4},{6,5},{7,6},{8,7},{9,8},{10,9},{11,1... | collective-permute-start | bytes 294920 | tf_op jit(solution)/shard_map/ppermute | solution.py:21
  76.0 1.6 %collective-permute-done = bf16[96,512]{1,0:T(8,128)(2,1)S(1)} collective-permute-done((bf16[96,512]{1,0:T(8,128)(2,1)S(1)}, bf16[96,512]{1,0:T(8,128)(2,1)S(1)}, u32[]{:S(2)}, u32[]{:S(2)}) %collective-permute-start) | collective-permute-done | bytes 98336 | tf_op jit(solution)/shard_map/ppermute | solution.py:18
  77.6 4.8 %gather_fusion.3 = bf16[1536,512]{1,0:T(8,128)(2,1)S(1)} fusion(bf16[288,512]{1,0:T(8,128)(2,1)S(1)} %pad_maximum_fusion, s32[2048]{0:T(1024)S(1)} %pad_clamp_fusion), kind=kCustom, calls=%fused_computation.3 | custom fusion | bytes 3151872 | tf_op jit(solution)/shard_map/jit(_take)/gather | solution.py:93
  82.5 6.0 %fusion.66 = (f32[1536]{0:T(1024)S(1)}, f32[1536,512]{1,0:T(8,128)}) fusion(bf16[512,512]{1,0:T(8,128)(2,1)} %param.33, f32[1536,512]{1,0:T(8,128)} %convolution_add_fusion.3, bf16[1536,512]{1,0:T(8,128)(2,1)S(1)} %gather_fusion.3, pred[1536]{0:T(1024)(128)(4,1)S(1)} %copy-done.17, bf16[1536,512]{1,0:T(8,128)(2,1)} %param.32), kind=kOutput, calls=%fused_computation.103 | convolution fusion | flops 1616902656 | bytes 8920576 | tf_op jit(solution)/shard_map/dot_general | solution.py:34
  88.5 2.6 %multiply_reduce_fusion = f32[1536]{0:T(1024)S(1)} fusion(f32[1536,512]{1,0:T(8,128)} %get-tuple-element.15, f32[1536]{0:T(1024)S(1)} %broadcast_multiply_fusion), kind=kLoop, calls=%fused_computation.9 | loop fusion | flops 2357760 | bytes 3158016 | tf_op jit(solution)/shard_map/reduce_sum | solution.py:28
  91.8 2.3 %reshape.82 = bf16[512,3,512]{2,1,0:T(4,128)(2,1)} reshape(bf16[1536,512]{1,0:T(8,128)(2,1)S(1)} %multiply_convert_fusion) | data formatting | bytes 3145728 | tf_op jit(solution)/shard_map/reshape | solution.py:104
  94.0 4.9 %reduce = bf16[512,512]{1,0:T(8,128)(2,1)} reduce(bf16[512,3,512]{2,1,0:T(4,128)(2,1)} %reshape.82, bf16[]{:T(256)} %constant.140), dimensions={1}, to_apply=%region_6.7.clone | reduce | flops 524288 | bytes 2097154 | tf_op jit(solution)/shard_map/reduce_sum | solution.py:103
  99.0 2.7 %fusion.71 = (f32[512]{0:T(512)S(1)}, f32[512,512]{0,1:T(8,128)S(1)}) fusion(bf16[512,512]{1,0:T(8,128)(2,1)} %param.35, f32[512,512]{1,0:T(8,128)} %fusion.26, bf16[512,512]{1,0:T(8,128)(2,1)} %reduce, bf16[1024,512]{1,0:T(8,128)(2,1)} %param.34), kind=kOutput, calls=%fused_computation.104 | convolution fusion | flops 538705408 | bytes 3672064 | tf_op jit(solution)/shard_map/dot_general | solution.py:34
  101.9 1.0 add_convert_fusion
  102.9 2.0 %copy.25 = bf16[512,512]{1,0:T(8,128)(2,1)} copy(bf16[512,512]{0,1:T(8,128)(2,1)} %add_convert_fusion) | data formatting | bytes 1048576
  (66 shorter events, 7.3 us)
Async XLA Ops:
  7.2 30.6 %copy-start = (bf16[1536,512]{1,0:T(8,128)(2,1)S(1)}, bf16[1536,512]{1,0:T(8,128)(2,1)}, u32[]{:S(2)}) copy-start(bf16[1536,512]{1,0:T(8,128)(2,1)} %param.26) | copy-start | bytes 4718596
  7.2 2.4 %copy-start.5 = (bf16[512,512]{1,0:T(8,128)(2,1)S(1)}, bf16[512,512]{1,0:T(8,128)(2,1)}, u32[]{:S(2)}) copy-start(bf16[512,512]{1,0:T(8,128)(2,1)} %param.25) | copy-start | bytes 1572868
  7.2 45.5 %all-gather.2.cloned.1.call-start = ((), (), s32[]{:S(2)}) async-start(), calls=%async_computation | async-start | bytes 1671168 | tf_op jit(solution)/shard_map/all_gather | solution.py:66
  13.3 6.0 %copy-start.13 = (s32[1152]{0:T(1024)S(1)}, s32[1152]{0:T(1024)}, u32[]{:S(2)}) copy-start(s32[1152]{0:T(1024)} %param.22) | copy-start | bytes 13828
  13.3 6.0 %copy-start.1 = (s32[16,8]{0,1:T(8,128)S(1)}, s32[16,8]{0,1:T(8,128)}, u32[]{:S(2)}) copy-start(s32[16,8]{0,1:T(8,128)} %param.24) | copy-start | bytes 1540
  19.3 5.0 %copy-start.12 = (s32[1152]{0:T(1024)S(1)}, s32[1152]{0:T(1024)}, u32[]{:S(2)}) copy-start(s32[1152]{0:T(1024)} %param.23) | copy-start | bytes 13828
  19.3 5.0 %copy-start.7 = (bf16[96,512]{1,0:T(8,128)(2,1)S(1)}, bf16[96,512]{1,0:T(8,128)(2,1)}, u32[]{:S(2)}) copy-start(bf16[96,512]{1,0:T(8,128)(2,1)} %param.20) | copy-start | bytes 294916
  25.6 4.4 %copy-start.14 = (s32[1536]{0:T(1024)S(1)}, s32[1536]{0:T(1024)}, u32[]{:S(2)}) copy-start(s32[1536]{0:T(1024)} %param.27) | copy-start | bytes 18436
  25.6 5.0 %copy-start.10 = (bf16[1024,512]{1,0:T(8,128)(2,1)S(1)}, bf16[1024,512]{1,0:T(8,128)(2,1)}, u32[]{:S(2)}) copy-start(bf16[1024,512]{1,0:T(8,128)(2,1)} %param.30) | copy-start | bytes 3145732
  29.9 4.1 %copy-start.4 = (f32[1152,512]{1,0:T(8,128)S(1)}, f32[1152,512]{1,0:T(8,128)}, u32[]{:S(2)}) copy-start(f32[1152,512]{1,0:T(8,128)} %gather_fusion) | copy-start | bytes 7077892
  34.0 3.8 %copy-start.2 = (f32[1536,512]{1,0:T(8,128)S(1)}, f32[1536,512]{1,0:T(8,128)}, u32[]{:S(2)}) copy-start(f32[1536,512]{1,0:T(8,128)} %reshape.81) | copy-start | bytes 9437188
  41.5 17.5 %copy-start.18 = (bf16[512,512]{1,0:T(8,128)(2,1)S(1)}, bf16[512,512]{1,0:T(8,128)(2,1)}, u32[]{:S(2)}) copy-start(bf16[512,512]{1,0:T(8,128)(2,1)} %param.29) | copy-start | bytes 1572868
  64.4 2.6 %copy-start.11 = (f32[96,512]{1,0:T(8,128)S(1)}, f32[96,512]{1,0:T(8,128)}, u32[]{:S(2)}) copy-start(f32[96,512]{1,0:T(8,128)} %fusion.34) | copy-start | bytes 589828
  66.4 3.1 %copy-start.8 = (bf16[512,512]{1,0:T(8,128)(2,1)S(1)}, bf16[512,512]{1,0:T(8,128)(2,1)}, u32[]{:S(2)}) copy-start(bf16[512,512]{1,0:T(8,128)(2,1)} %param.31) | copy-start | bytes 1572868
  70.8 11.7 %copy-start.9 = (bf16[96,512]{1,0:T(8,128)(2,1)}, bf16[96,512]{1,0:T(8,128)(2,1)S(1)}, u32[]{:S(2)}) copy-start(bf16[96,512]{1,0:T(8,128)(2,1)S(1)} %add_convert_fusion.1) | copy-start | bytes 294916
  70.8 6.8 %collective-permute-start = (bf16[96,512]{1,0:T(8,128)(2,1)S(1)}, bf16[96,512]{1,0:T(8,128)(2,1)S(1)}, u32[]{:S(2)}, u32[]{:S(2)}) collective-permute-start(bf16[96,512]{1,0:T(8,128)(2,1)S(1)} %add_convert_fusion.1), channel_id=1, source_target_pairs={{0,1},{1,2},{2,3},{3,4},{4,5},{5,6},{6,7},{7,8},{8,9},{9,10},{10,1... | collective-permute-start | bytes 294920 | tf_op jit(solution)/shard_map/ppermute | solution.py:18
  71.1 6.5 %collective-permute-start.1 = (bf16[96,512]{1,0:T(8,128)(2,1)S(1)}, bf16[96,512]{1,0:T(8,128)(2,1)S(1)}, u32[]{:S(2)}, u32[]{:S(2)}) collective-permute-start(bf16[96,512]{1,0:T(8,128)(2,1)S(1)} %add_convert_fusion.1), channel_id=1, source_target_pairs={{1,0},{2,1},{3,2},{4,3},{5,4},{6,5},{7,6},{8,7},{9,8},{10,9},{11,1... | collective-permute-start | bytes 294920 | tf_op jit(solution)/shard_map/ppermute | solution.py:21
  77.6 4.8 %copy-start.17 = (pred[1536]{0:T(1024)(128)(4,1)S(1)}, pred[1536]{0:T(1024)(128)(4,1)}, u32[]{:S(2)}) copy-start(pred[1536]{0:T(1024)(128)(4,1)} %get-tuple-element.6) | copy-start | bytes 4612
  88.4 2.8 %copy-start.3 = (f32[1536,512]{1,0:T(8,128)S(1)}, f32[1536,512]{1,0:T(8,128)}, u32[]{:S(2)}) copy-start(f32[1536,512]{1,0:T(8,128)} %get-tuple-element.15) | copy-start | bytes 9437188
  88.5 2.8 %copy-start.15 = (f32[512]{0:T(512)S(1)}, f32[512]{0:T(512)}, u32[]{:S(2)}) copy-start(f32[512]{0:T(512)} %param.38) | copy-start | bytes 6148
  99.0 2.9 %copy-start.6 = (bf16[512,512]{0,1:T(8,128)(2,1)S(1)}, bf16[512,512]{0,1:T(8,128)(2,1)}, u32[]{:S(2)}) copy-start(bf16[512,512]{0,1:T(8,128)(2,1)} %copy.24) | copy-start | bytes 1572868
  99.0 2.9 %copy-start.16 = (f32[512]{0:T(512)S(1)}, f32[512]{0:T(512)}, u32[]{:S(2)}) copy-start(f32[512]{0:T(512)} %param.39) | copy-start | bytes 6148
Sparse Core Ops, SparseCore 0:
  10.3 42.3 all-gather.1
where the time goes:
time: 112 us
  local copies, waits for them, and re-layouts  34.7 us (31%)
  matrix products  30.6 us (27%)
  between operations  14.3 us (13%)
  other arithmetic  14.2 us (13%)
  waiting for transfers between devices  13.5 us (12%)
  starting transfers between devices  4.53 us (4%)
    dot_general x4, matrix products, second_layer(): jnp.dot(hidden, w_second, preferred_element_type=jnp.float32)  14.4 us
    all_gather x1, waiting for transfers between devices, local(): gathered = lax.all_gather(mesh_latent, 'lon', axis=0, tiled=True)  11.2 us
    gather x1, local copies, waits for them, and re-layouts, local(): senders = jnp.take(gathered, sender_id, axis=0)  6.34 us
    reshape x1, local copies, waits for them, and re-layouts, local(): grid_sum = grid_sum + jnp.repeat(grid_receiver_term, NEAR, axis=0)  5.95 us
    reduce_sum x1, other arithmetic, local(): jnp.sum(grid_message.astype(jnp.float32).reshape(grid_latent.shape[0], NE...  4.95 us
    gather x1, local copies, waits for them, and re-layouts, local(): sender_id = owner_dev * rows_mesh + proc_lists[owner_dev, list_col]  4.94 us
    reduce_sum x4, other arithmetic, layer_norm(): spread = jnp.mean(center * center, axis=-1, keepdims=True)  4.91 us
    gather x1, local copies, waits for them, and re-layouts, local(): grid_senders = jnp.take(window, place, axis=0)  4.81 us
  transfers between devices with their start and end apart: 3, of which 2 were waited for; matrix products, arithmetic and copies ran while one was open for 31% of the time, Pallas kernels for 0%

commit v1 on v0

v1 whole, which is shorter than its diff:
```python
import functools

import jax
import jax.numpy as jnp
from jax import lax
from jax.experimental import pallas as pl
from jax.experimental.pallas import tpu as pltpu
from jax.sharding import PartitionSpec as P

NEAR = 3
EPSILON = 1e-05
BLOCK = 384
LANES = 128
BF16 = jnp.bfloat16
F32 = jnp.float32
MESH_ID = pl.DeviceIdType.MESH


def mm(a, b):
    return jnp.dot(a, b, preferred_element_type=F32)


def mm_t(a, b):
    return lax.dot_general(a, b, (((0,), (0,)), ((), ())), preferred_element_type=F32)


def pick(flags):
    return jnp.where(flags, 1.0, 0.0).astype(BF16)


def act(first_sum):
    half = 0.5 * first_sum
    return (half + half * jnp.tanh(half)).astype(BF16)


def norm(values, gain):
    center = values - jnp.mean(values, axis=-1, keepdims=True)
    spread = jnp.mean(center * center, axis=-1, keepdims=True)
    return center * lax.rsqrt(spread + EPSILON) * gain


def iota(shape, dim):
    return lax.broadcasted_iota(jnp.int32, shape, dim)


def kernel(
    n,
    lat,
    slot,
    recv,
    lists,
    gsend,
    pe_gain,
    pn_gain,
    ge_gain,
    gn_gain,
    *refs,
):
    hbm = refs[:11]
    mesh_out, grid_out = refs[11:13]
    vm = refs[13:24]
    (
        list_src,
        list_dst,
        rows_src,
        rows_dst,
        term_pad,
        table,
        edge_acc,
        grid_acc,
        gnode_acc,
        incoming,
        own_term,
        side_term,
        gin,
        load_sem,
        list_send,
        list_recv,
        rows_send,
        rows_recv,
        side_send,
        side_recv,
    ) = refs[24:]
    edges, glat, gedges, pe_in, pe_out, pn_in, pn_out, ge_in, ge_out, gn_in, gn_out = vm
    order = (3, 0, 5, 7, 2, 1, 9, 4, 6, 8, 10)

    def load(k):
        return pltpu.make_async_copy(hbm[k], vm[k], load_sem.at[k])

    for k in order:
        load(k).start()

    me = lax.axis_index("lon")
    rows, width = lat.shape
    cap = lists.shape[1]
    half = width // 2
    n_tab = n * cap
    n_edges = edges.shape[0]
    n_gedges = gedges.shape[0]
    n_grid = glat.shape[0]
    nodes = BLOCK // NEAR

    def at(distance):
        return lax.rem(me + distance + n, n)

    barrier = pltpu.get_barrier_semaphore()

    def greet(d, carry):
        pl.semaphore_signal(barrier, inc=1, device_id={"lon": at(d)}, device_id_type=MESH_ID)
        return carry

    lax.fori_loop(1, n, greet, 0)

    def spread_list(o, carry):
        row = jnp.broadcast_to(lists[pl.ds(o, 1), :].astype(F32), (cap, cap))
        kept = jnp.where(iota((cap, cap), 0) == iota((cap, cap), 1), row, 0.0)
        column = jnp.sum(kept, axis=1, keepdims=True)
        list_src[o] = jnp.broadcast_to(column, (cap, LANES)).astype(jnp.int32)
        return carry

    lax.fori_loop(0, n, spread_list, 0)
    pl.semaphore_wait(barrier, n - 1)

    def list_copy(d):
        return pltpu.make_async_remote_copy(
            src_ref=list_src.at[at(d)],
            dst_ref=list_dst.at[d],
            send_sem=list_send,
            recv_sem=list_recv,
            device_id={"lon": at(d)},
            device_id_type=MESH_ID,
        )

    def send_list(d, carry):
        list_copy(d).start()
        return carry

    lax.fori_loop(1, n, send_list, 0)
    list_dst[0] = list_src[me]

    load(3).wait()
    lat_v = lat[...]
    term_pad[...] = jnp.zeros_like(term_pad)
    term_pad[0:rows, :] = mm(lat_v, pe_in[width : 2 * width, :]).astype(BF16)
    table[n_tab:, :] = jnp.zeros((LANES, width), BF16)
    table[n_tab : n_tab + rows, :] = mm(lat_v, pe_in[2 * width :, :]).astype(BF16)

    load(0).wait()

    def edge_first(b, carry):
        here = pl.ds(pl.multiple_of(b * BLOCK, BLOCK), BLOCK)
        edge_acc[here, :] = mm(edges[here, :], pe_in[0:width, :])
        return carry

    lax.fori_loop(0, n_edges // BLOCK, edge_first, 0)

    got = list_dst.at[pl.ds(1, n - 1)]
    pltpu.make_async_copy(got, got, list_recv).wait()
    wanted = list_dst[...].reshape(n_tab, LANES)
    chosen = pick(wanted == iota((n_tab, LANES), 1))
    left_half = mm(chosen, term_pad[:, 0:half]).reshape(n, cap, half)
    right_half = mm(chosen, term_pad[:, half:]).reshape(n, cap, half)
    rows_src[...] = (
        jnp.concatenate([left_half, right_half], axis=1).reshape(n_tab * 2, half).astype(BF16)
    )
    chunk = 2 * cap

    def rows_copy(d):
        return pltpu.make_async_remote_copy(
            src_ref=rows_src.at[pl.ds(pl.multiple_of(d * chunk, chunk), chunk), :],
            dst_ref=rows_dst.at[pl.ds(pl.multiple_of((n - d) * chunk, chunk), chunk), :],
            send_sem=rows_send,
            recv_sem=rows_recv,
            device_id={"lon": at(-d)},
            device_id_type=MESH_ID,
        )

    def send_rows(d, carry):
        rows_copy(d).start()
        return carry

    lax.fori_loop(1, n, send_rows, 0)
    rows_dst[0:chunk, :] = rows_src[0:chunk, :]

    load(5).wait()
    load(7).wait()
    load(2).wait()
    load(1).wait()
    node_own = mm(lat_v, pn_in[0:width, :])
    repeat = pick(iota((BLOCK, nodes), 0) // NEAR == iota((BLOCK, nodes), 1))

    def grid_first(b, carry):
        here = pl.ds(pl.multiple_of(b * BLOCK, BLOCK), BLOCK)
        there = pl.ds(pl.multiple_of(b * nodes, nodes), nodes)
        term = mm(glat[there, :], ge_in[2 * width :, :]).astype(BF16)
        grid_acc[here, :] = mm(gedges[here, :], ge_in[0:width, :]) + mm(repeat, term)
        return carry

    lax.fori_loop(0, n_gedges // BLOCK, grid_first, 0)
    load(9).wait()
    gnode_acc[...] = mm(glat[...], gn_in[0:width, :])
    load(4).wait()
    load(6).wait()

    arrived = rows_dst.at[pl.ds(chunk, (n - 1) * chunk), :]
    pltpu.make_async_copy(arrived, arrived, rows_recv).wait()
    parts = rows_dst[...].astype(F32).reshape(n, 2, cap, half)
    table[0:n_tab, :] = jnp.concatenate(
        [parts[:, 0].reshape(n_tab, half), parts[:, 1].reshape(n_tab, half)], axis=1
    ).astype(BF16)

    distance = me - iota((n, cap, BLOCK), 0)
    owner = jnp.where(distance < 0, distance + n, distance)
    slot_of = (owner * cap + iota((n, cap, BLOCK), 1)).reshape(n_tab, BLOCK)
    incoming[...] = jnp.zeros_like(incoming)

    def edge_second(b, carry):
        here = pl.ds(pl.multiple_of(b * BLOCK, BLOCK), BLOCK)
        slots = slot[:, here]
        receivers = recv[:, here]
        gather = jnp.concatenate(
            [
                pick(slot_of == slots),
                pick(iota((LANES, BLOCK), 0) == jnp.minimum(receivers, rows - 1)),
            ],
            axis=0,
        )
        total = edge_acc[here, :] + mm_t(gather, table[...])
        message = norm(mm(act(total), pe_out[...]), pe_gain[...]).astype(BF16)
        incoming[...] += mm(pick(iota((rows, BLOCK), 0) == receivers), message)
        return carry

    lax.fori_loop(0, n_edges // BLOCK, edge_second, 0)

    node_sum = node_own + mm(incoming[...].astype(BF16), pn_in[width:, :])
    mesh_new = (
        lat_v.astype(F32) + norm(mm(act(node_sum), pn_out[...]), pn_gain[...])
    ).astype(BF16)
    mesh_out[...] = mesh_new
    own_term[...] = mm(mesh_new, ge_in[width : 2 * width, :]).astype(BF16)

    def side_copy(side):
        return pltpu.make_async_remote_copy(
            src_ref=own_term,
            dst_ref=side_term.at[pl.ds(side * rows, rows), :],
            send_sem=side_send.at[side],
            recv_sem=side_recv.at[side],
            device_id={"lon": at(1 - 2 * side)},
            device_id_type=MESH_ID,
        )

    side_copy(0).start()
    side_copy(1).start()
    load(8).wait()
    load(10).wait()

    def grid_own(b, carry):
        here = pl.ds(pl.multiple_of(b * BLOCK, BLOCK), BLOCK)
        gather = pick(iota((rows, BLOCK), 0) + me * rows == gsend[:, here])
        grid_acc[here, :] += mm_t(gather, own_term[...])
        return carry

    lax.fori_loop(0, n_gedges // BLOCK, grid_own, 0)
    side_copy(0).wait_recv()
    side_copy(1).wait_recv()
    pooled = pick(iota((nodes, BLOCK), 1) // NEAR == iota((nodes, BLOCK), 0))
    side_index = jnp.concatenate(
        [iota((rows, BLOCK), 0) + at(-1) * rows, iota((rows, BLOCK), 0) + at(1) * rows], axis=0
    )

    def grid_second(b, carry):
        here = pl.ds(pl.multiple_of(b * BLOCK, BLOCK), BLOCK)
        there = pl.ds(pl.multiple_of(b * nodes, nodes), nodes)
        gather = pick(side_index == gsend[:, here])
        total = grid_acc[here, :] + mm_t(gather, side_term[...])
        message = norm(mm(act(total), ge_out[...]), ge_gain[...]).astype(BF16)
        gin[there, :] = mm(pooled, message).astype(BF16)
        return carry

    lax.fori_loop(0, n_gedges // BLOCK, grid_second, 0)

    def grid_node(b, carry):
        there = pl.ds(pl.multiple_of(b * (n_grid // 2), n_grid // 2), n_grid // 2)
        total = gnode_acc[there, :] + mm(gin[there, :], gn_in[width:, :])
        update = norm(mm(act(total), gn_out[...]), gn_gain[...])
        grid_out[there, :] = (glat[there, :].astype(F32) + update).astype(BF16)
        return carry

    lax.fori_loop(0, 2, grid_node, 0)

    sent = list_src.at[pl.ds(1, n - 1)]
    pltpu.make_async_copy(sent, sent, list_send).wait()
    gone = rows_src.at[pl.ds(chunk, (n - 1) * chunk), :]
    pltpu.make_async_copy(gone, gone, rows_send).wait()
    side_copy(0).wait_send()
    side_copy(1).wait_send()


def local(
    mesh_latent,
    mesh_edges,
    proc_slot,
    proc_receiver,
    proc_lists,
    grid_latent,
    grid_edges,
    grid_sender,
    proc_edge_in,
    proc_edge_out,
    proc_node_in,
    proc_node_out,
    grid_edge_in,
    grid_edge_out,
    grid_node_in,
    grid_node_out,
    proc_edge_gain,
    proc_node_gain,
    grid_edge_gain,
    grid_node_gain,
):
    n = lax.axis_size("lon")
    rows, width = mesh_latent.shape
    cap = proc_lists.shape[1]
    n_tab = n * cap
    n_edges = mesh_edges.shape[0]
    n_gedges = grid_edges.shape[0]
    n_grid = grid_latent.shape[0]
    big = (
        mesh_edges,
        grid_latent,
        grid_edges,
        proc_edge_in,
        proc_edge_out,
        proc_node_in,
        proc_node_out,
        grid_edge_in,
        grid_edge_out,
        grid_node_in,
        grid_node_out,
    )
    small = (
        mesh_latent,
        proc_slot.reshape(1, -1),
        proc_receiver.reshape(1, -1),
        proc_lists,
        grid_sender.reshape(1, -1),
        proc_edge_gain.reshape(1, -1),
        proc_node_gain.reshape(1, -1),
        grid_edge_gain.reshape(1, -1),
        grid_node_gain.reshape(1, -1),
    )
    vmem = pl.BlockSpec(memory_space=pltpu.VMEM)
    return pl.pallas_call(
        functools.partial(kernel, n),
        out_shape=(
            jax.ShapeDtypeStruct(mesh_latent.shape, BF16),
            jax.ShapeDtypeStruct(grid_latent.shape, BF16),
        ),
        in_specs=[vmem] * len(small) + [pl.BlockSpec(memory_space=pl.ANY)] * len(big),
        out_specs=(vmem, vmem),
        scratch_shapes=[pltpu.VMEM(a.shape, a.dtype) for a in big]
        + [
            pltpu.VMEM((n, cap, LANES), jnp.int32),
            pltpu.VMEM((n, cap, LANES), jnp.int32),
            pltpu.VMEM((n_tab * 2, width // 2), BF16),
            pltpu.VMEM((n_tab * 2, width // 2), BF16),
            pltpu.VMEM((LANES, width), BF16),
            pltpu.VMEM((n_tab + LANES, width), BF16),
            pltpu.VMEM((n_edges, width), F32),
            pltpu.VMEM((n_gedges, width), F32),
            pltpu.VMEM((n_grid, width), F32),
            pltpu.VMEM((rows, width), F32),
            pltpu.VMEM((rows, width), BF16),
            pltpu.VMEM((2 * rows, width), BF16),
            pltpu.VMEM((n_grid, width), BF16),
            pltpu.SemaphoreType.DMA((len(big),)),
            pltpu.SemaphoreType.DMA,
            pltpu.SemaphoreType.DMA,
            pltpu.SemaphoreType.DMA,
            pltpu.SemaphoreType.DMA,
            pltpu.SemaphoreType.DMA((2,)),
            pltpu.SemaphoreType.DMA((2,)),
        ],
        compiler_params=pltpu.CompilerParams(
            collective_id=0, has_side_effects=True, vmem_limit_bytes=50 * 1024 * 1024
        ),
    )(*small, *big)


def solution(mesh):
    rows = P(("groups", "lon"), None)
    flat = P(("groups", "lon"))
    placed = (rows, rows, flat, flat, rows, rows, rows, flat) + (P(),) * 12
    return jax.shard_map(
        local,
        mesh=mesh,
        in_specs=placed,
        out_specs=(rows, rows),
        check_vma=False,
    )
```

time: 112 us -> 42.6 us (0.38)
  the two profiles are of different devices: /device:TPU:0 before, /device:TPU:1 now
where the time goes in v1:
time: 42.6 us; the launch traced here: 42 us
  Pallas kernels  28.2 us (66%)
  local copies, waits for them, and re-layouts  13.1 us (31%)
  between operations  0.65 us (2%)
    pallas_call x1, Pallas kernels, local(): pl.pallas_call(functools.partial(kernel, n), out_shape=(jax.ShapeDtypeStr...  28.2 us
    unnamed x23, local copies, waits for them, and re-layouts  11 us

profile of v1, /device:TPU:1, one launch (start us, length us, event | category | flops | bytes accessed | tf_op | source)
XLA Modules:
  0.0 42.0 jit_solution(6060083446543877567)
XLA Ops:
  0.6 0.7 %reshape.25.slot = s32[1,1152]{1,0:T(1,128)S(1)} reshape(s32[1152]{0:T(1024)} %param.22) | data formatting | bytes 9216 | tf_op jit(solution)/shard_map/reshape | solution.py:343
  1.3 0.7 %reshape.26.recv = s32[1,1152]{1,0:T(1,128)S(1)} reshape(s32[1152]{0:T(1024)} %param.23) | data formatting | bytes 9216 | tf_op jit(solution)/shard_map/reshape | solution.py:344
  2.0 0.7 %reshape.27.gsend = s32[1,1536]{1,0:T(1,128)S(1)} reshape(s32[1536]{0:T(1024)} %param.27) | data formatting | bytes 12288 | tf_op jit(solution)/shard_map/reshape | solution.py:346
  2.7 0.8 %copy.22.lists = s32[16,8]{1,0:T(8,128)S(1)} copy(s32[16,8]{0,1:T(8,128)} %param.24) | data formatting | bytes 1024 | tf_op args[4]
  3.5 0.0 copy-start
  3.5 1.0 %copy-done = bf16[512,512]{1,0:T(8,128)(2,1)S(1)} copy-done((bf16[512,512]{1,0:T(8,128)(2,1)S(1)}, bf16[512,512]{1,0:T(8,128)(2,1)}, u32[]{:S(2)}) %copy-start) | copy-done | bytes 524312
  4.5 0.0 copy-start.1
  4.5 1.0 %copy-done.1 = bf16[512,512]{1,0:T(8,128)(2,1)S(1)} copy-done((bf16[512,512]{1,0:T(8,128)(2,1)S(1)}, bf16[512,512]{1,0:T(8,128)(2,1)}, u32[]{:S(2)}) %copy-start.1) | copy-done | bytes 524312
  5.6 0.0 copy-start.2
  5.6 1.0 %copy-done.2 = bf16[512,512]{1,0:T(8,128)(2,1)S(1)} copy-done((bf16[512,512]{1,0:T(8,128)(2,1)S(1)}, bf16[512,512]{1,0:T(8,128)(2,1)}, u32[]{:S(2)}) %copy-start.2) | copy-done | bytes 524312
  6.6 0.0 copy-start.3
  6.6 1.0 %copy-done.3 = bf16[512,512]{1,0:T(8,128)(2,1)S(1)} copy-done((bf16[512,512]{1,0:T(8,128)(2,1)S(1)}, bf16[512,512]{1,0:T(8,128)(2,1)}, u32[]{:S(2)}) %copy-start.3) | copy-done | bytes 524312
  7.7 0.0 copy-start.4
  7.7 1.0 %copy-done.4 = bf16[512,512]{1,0:T(8,128)(2,1)S(1)} copy-done((bf16[512,512]{1,0:T(8,128)(2,1)S(1)}, bf16[512,512]{1,0:T(8,128)(2,1)}, u32[]{:S(2)}) %copy-start.4) | copy-done | bytes 524312
  8.7 0.0 copy-start.5
  8.7 0.9 %copy-done.5 = bf16[96,512]{1,0:T(8,128)(2,1)S(1)} copy-done((bf16[96,512]{1,0:T(8,128)(2,1)S(1)}, bf16[96,512]{1,0:T(8,128)(2,1)}, u32[]{:S(2)}) %copy-start.5) | copy-done | bytes 98328
  9.6 0.0 copy-start.6
  9.6 0.7 %copy-done.6 = f32[512]{0:T(512)S(1)} copy-done((f32[512]{0:T(512)S(1)}, f32[512]{0:T(512)}, u32[]{:S(2)}) %copy-start.6) | copy-done | bytes 2072
  10.3 0.7 %copy-done.7 = f32[512]{0:T(512)S(1)} copy-done((f32[512]{0:T(512)S(1)}, f32[512]{0:T(512)}, u32[]{:S(2)}) %copy-start.7) | copy-done | bytes 2072
  11.0 0.7 %copy-done.8 = f32[512]{0:T(512)S(1)} copy-done((f32[512]{0:T(512)S(1)}, f32[512]{0:T(512)}, u32[]{:S(2)}) %copy-start.8) | copy-done | bytes 2072
  11.6 0.7 %copy-done.9 = f32[512]{0:T(512)S(1)} copy-done((f32[512]{0:T(512)S(1)}, f32[512]{0:T(512)}, u32[]{:S(2)}) %copy-start.9) | copy-done | bytes 2072
  12.3 28.2 %shard_map.203 = (bf16[96,512]{1,0:T(8,128)(2,1)S(1)}, bf16[512,512]{1,0:T(8,128)(2,1)S(1)}) custom-call(bf16[96,512]{1,0:T(8,128)(2,1)S(1)} %copy-done.5, s32[1,1152]{1,0:T(1,128)S(1)} %reshape.25.slot, s32[1,1152]{1,0:T(1,128)S(1)} %reshape.26.recv, s32[16,8]{1,0:T(8,128)S(1)} %copy.22.lists, s32[1,1536]{1,0:T(1,128)S(1)} %reshape.27.gsend, ...), custom_call_target="tpu_custom_call" | custom-call | tf_op jit(solution)/shard_map/pallas_call | solution.py:353
  40.5 0.6 %copy.25 = bf16[96,512]{1,0:T(8,128)(2,1)} copy(bf16[96,512]{1,0:T(8,128)(2,1)S(1)} %get-tuple-element.4) | data formatting | bytes 196608
  41.2 0.8 %copy.26 = bf16[512,512]{1,0:T(8,128)(2,1)} copy(bf16[512,512]{1,0:T(8,128)(2,1)S(1)} %get-tuple-element.5) | data formatting | bytes 1048576
  (3 shorter events, 0.0 us)
Async XLA Ops:
  3.5 1.0 %copy-start = (bf16[512,512]{1,0:T(8,128)(2,1)S(1)}, bf16[512,512]{1,0:T(8,128)(2,1)}, u32[]{:S(2)}) copy-start(bf16[512,512]{1,0:T(8,128)(2,1)} %refs_1_.1) | copy-start | bytes 1572868
  4.5 1.0 %copy-start.1 = (bf16[512,512]{1,0:T(8,128)(2,1)S(1)}, bf16[512,512]{1,0:T(8,128)(2,1)}, u32[]{:S(2)}) copy-start(bf16[512,512]{1,0:T(8,128)(2,1)} %refs_4_.1) | copy-start | bytes 1572868
  5.6 1.0 %copy-start.2 = (bf16[512,512]{1,0:T(8,128)(2,1)S(1)}, bf16[512,512]{1,0:T(8,128)(2,1)}, u32[]{:S(2)}) copy-start(bf16[512,512]{1,0:T(8,128)(2,1)} %refs_6_.1) | copy-start | bytes 1572868
  6.6 1.0 %copy-start.3 = (bf16[512,512]{1,0:T(8,128)(2,1)S(1)}, bf16[512,512]{1,0:T(8,128)(2,1)}, u32[]{:S(2)}) copy-start(bf16[512,512]{1,0:T(8,128)(2,1)} %refs_8_.1) | copy-start | bytes 1572868
  7.7 1.0 %copy-start.4 = (bf16[512,512]{1,0:T(8,128)(2,1)S(1)}, bf16[512,512]{1,0:T(8,128)(2,1)}, u32[]{:S(2)}) copy-start(bf16[512,512]{1,0:T(8,128)(2,1)} %refs_10_.1) | copy-start | bytes 1572868
  8.7 0.9 %copy-start.5 = (bf16[96,512]{1,0:T(8,128)(2,1)S(1)}, bf16[96,512]{1,0:T(8,128)(2,1)}, u32[]{:S(2)}) copy-start(bf16[96,512]{1,0:T(8,128)(2,1)} %lat.1) | copy-start | bytes 294916
  9.6 0.7 %copy-start.6 = (f32[512]{0:T(512)S(1)}, f32[512]{0:T(512)}, u32[]{:S(2)}) copy-start(f32[512]{0:T(512)} %param.36) | copy-start | bytes 6148
  10.3 0.7 %copy-start.7 = (f32[512]{0:T(512)S(1)}, f32[512]{0:T(512)}, u32[]{:S(2)}) copy-start(f32[512]{0:T(512)} %param.37) | copy-start | bytes 6148
  11.0 0.7 %copy-start.8 = (f32[512]{0:T(512)S(1)}, f32[512]{0:T(512)}, u32[]{:S(2)}) copy-start(f32[512]{0:T(512)} %param.38) | copy-start | bytes 6148
  11.6 0.7 %copy-start.9 = (f32[512]{0:T(512)S(1)}, f32[512]{0:T(512)}, u32[]{:S(2)}) copy-start(f32[512]{0:T(512)} %param.39) | copy-start | bytes 6148

commit v2 on v1

--- a/solution.py
+++ b/solution.py
@@ -45,21 +45,15 @@
 
 def kernel(
     n,
-    lat,
-    slot,
-    recv,
-    lists,
-    gsend,
-    pe_gain,
-    pn_gain,
-    ge_gain,
-    gn_gain,
     *refs,
 ):
-    hbm = refs[:11]
-    mesh_out, grid_out = refs[11:13]
-    vm = refs[13:24]
+    hbm = refs[:20]
+    mesh_out, grid_out = refs[20:22]
+    vm = refs[22:42]
     (
+        slot,
+        recv,
+        gsend,
         list_src,
         list_dst,
         rows_src,
@@ -80,9 +74,10 @@
         rows_recv,
         side_send,
         side_recv,
-    ) = refs[24:]
-    edges, glat, gedges, pe_in, pe_out, pn_in, pn_out, ge_in, ge_out, gn_in, gn_out = vm
-    order = (3, 0, 5, 7, 2, 1, 9, 4, 6, 8, 10)
+    ) = refs[42:]
+    edges, glat, gedges, pe_in, pe_out, pn_in, pn_out, ge_in, ge_out, gn_in, gn_out = vm[:11]
+    lat, lists, slot_flat, recv_flat, gsend_flat, pe_gain, pn_gain, ge_gain, gn_gain = vm[11:]
+    order = (12, 11, 3, 0, 13, 14, 5, 7, 2, 1, 9, 4, 6, 15, 16, 17, 18, 19, 8, 10)
 
     def load(k):
         return pltpu.make_async_copy(hbm[k], vm[k], load_sem.at[k])
@@ -92,7 +87,7 @@
 
     me = lax.axis_index("lon")
     rows, width = lat.shape
-    cap = lists.shape[1]
+    cap = lists.shape[0]
     half = width // 2
     n_tab = n * cap
     n_edges = edges.shape[0]
@@ -112,12 +107,12 @@
     lax.fori_loop(1, n, greet, 0)
 
     def spread_list(o, carry):
-        row = jnp.broadcast_to(lists[pl.ds(o, 1), :].astype(F32), (cap, cap))
-        kept = jnp.where(iota((cap, cap), 0) == iota((cap, cap), 1), row, 0.0)
+        kept = jnp.where(iota((cap, n), 1) == o, lists[...].astype(F32), 0.0)
         column = jnp.sum(kept, axis=1, keepdims=True)
         list_src[o] = jnp.broadcast_to(column, (cap, LANES)).astype(jnp.int32)
         return carry
 
+    load(12).wait()
     lax.fori_loop(0, n, spread_list, 0)
     pl.semaphore_wait(barrier, n - 1)
 
@@ -138,6 +133,7 @@
     lax.fori_loop(1, n, send_list, 0)
     list_dst[0] = list_src[me]
 
+    load(11).wait()
     load(3).wait()
     lat_v = lat[...]
     term_pad[...] = jnp.zeros_like(term_pad)
@@ -182,8 +178,10 @@
     lax.fori_loop(1, n, send_rows, 0)
     rows_dst[0:chunk, :] = rows_src[0:chunk, :]
 
-    load(5).wait()
-    load(7).wait()
+    for k in (13, 14, 5, 7):
+        load(k).wait()
+    slot[...] = slot_flat[...].reshape(1, n_edges)
+    recv[...] = recv_flat[...].reshape(1, n_edges)
     load(2).wait()
     load(1).wait()
     node_own = mm(lat_v, pn_in[0:width, :])
@@ -199,8 +197,9 @@
     lax.fori_loop(0, n_gedges // BLOCK, grid_first, 0)
     load(9).wait()
     gnode_acc[...] = mm(glat[...], gn_in[0:width, :])
-    load(4).wait()
-    load(6).wait()
+    for k in (4, 6, 15, 16, 17, 18, 19):
+        load(k).wait()
+    gsend[...] = gsend_flat[...].reshape(1, n_gedges)
 
     arrived = rows_dst.at[pl.ds(chunk, (n - 1) * chunk), :]
     pltpu.make_async_copy(arrived, arrived, rows_recv).wait()
@@ -340,10 +339,10 @@
     )
     small = (
         mesh_latent,
-        proc_slot.reshape(1, -1),
-        proc_receiver.reshape(1, -1),
-        proc_lists,
-        grid_sender.reshape(1, -1),
+        proc_lists.T,
+        proc_slot,
+        proc_receiver,
+        grid_sender,
         proc_edge_gain.reshape(1, -1),
         proc_node_gain.reshape(1, -1),
         grid_edge_gain.reshape(1, -1),
@@ -356,10 +355,13 @@
             jax.ShapeDtypeStruct(mesh_latent.shape, BF16),
             jax.ShapeDtypeStruct(grid_latent.shape, BF16),
         ),
-        in_specs=[vmem] * len(small) + [pl.BlockSpec(memory_space=pl.ANY)] * len(big),
+        in_specs=[pl.BlockSpec(memory_space=pltpu.HBM)] * len(big + small),
         out_specs=(vmem, vmem),
-        scratch_shapes=[pltpu.VMEM(a.shape, a.dtype) for a in big]
+        scratch_shapes=[pltpu.VMEM(a.shape, a.dtype) for a in big + small]
         + [
+            pltpu.VMEM((1, n_edges), jnp.int32),
+            pltpu.VMEM((1, n_edges), jnp.int32),
+            pltpu.VMEM((1, n_gedges), jnp.int32),
             pltpu.VMEM((n, cap, LANES), jnp.int32),
             pltpu.VMEM((n, cap, LANES), jnp.int32),
             pltpu.VMEM((n_tab * 2, width // 2), BF16),
@@ -373,7 +375,7 @@
             pltpu.VMEM((rows, width), BF16),
             pltpu.VMEM((2 * rows, width), BF16),
             pltpu.VMEM((n_grid, width), BF16),
-            pltpu.SemaphoreType.DMA((len(big),)),
+            pltpu.SemaphoreType.DMA((len(big + small),)),
             pltpu.SemaphoreType.DMA,
             pltpu.SemaphoreType.DMA,
             pltpu.SemaphoreType.DMA,
@@ -382,9 +384,9 @@
             pltpu.SemaphoreType.DMA((2,)),
         ],
         compiler_params=pltpu.CompilerParams(
-            collective_id=0, has_side_effects=True, vmem_limit_bytes=50 * 1024 * 1024
+            collective_id=0, has_side_effects=True, vmem_limit_bytes=62 * 1024 * 1024
         ),
-    )(*small, *big)
+    )(*big, *small)
 
 
 def solution(mesh):

time: 42.6 us -> 33.3 us (0.78); the launches traced: 42 us -> 33.1 us
  local copies, waits for them, and re-layouts: 13.1 us -> 3.41 us
  Pallas kernels: 28.2 us -> 29.1 us
    unnamed x23 -> x2, local copies, waits for them, and re-layouts: 11 us -> 3.41 us
    reshape x3 -> x0, local copies, waits for them, and re-layouts: 2.1 us -> none  [the longest x1 0.7 us: local(): proc_slot.reshape(1, -1)]
    pallas_call x1, Pallas kernels: 28.2 us -> 29.1 us  [local(): pl.pallas_call(functools.partial(kernel, n), out_shape=(jax.ShapeDtypeStr...]
where the time goes in v2:
time: 33.3 us; the launch traced here: 33.1 us
  Pallas kernels  29.1 us (87%)
  local copies, waits for them, and re-layouts  3.41 us (10%)
  between operations  0.65 us (2%)
    pallas_call x1, Pallas kernels, local(): pl.pallas_call(functools.partial(kernel, n), out_shape=(jax.ShapeDtypeStr...  29.1 us
    unnamed x2, local copies, waits for them, and re-layouts  3.41 us

profile of v2, /device:TPU:1, one launch (start us, length us, event | category | flops | bytes accessed | tf_op | source)
XLA Modules:
  0.0 33.1 jit_solution(14277020454295286887)
XLA Ops:
  0.6 29.1 %shard_map.203 = (bf16[96,512]{1,0:T(8,128)(2,1)}, bf16[512,512]{1,0:T(8,128)(2,1)}) custom-call(bf16[1152,512]{1,0:T(8,128)(2,1)} %refs_0_.1, bf16[512,512]{1,0:T(8,128)(2,1)} %refs_1_.1, bf16[1536,512]{1,0:T(8,128)(2,1)} %refs_2_.1, bf16[1536,512]{1,0:T(8,128)(2,1)} %refs_3_.1, bf16[512,512]{1,0:T(8,128)(2,1)} %refs_4_.1, bf16[1024,512]{1,0:T(8,128)(2,1)} %refs_5_.1, ...), custom_call_target="tpu_custom_call" | custom-call | tf_op jit(solution)/shard_map/pallas_call | solution.py:352
  29.7 1.5 %copy.24 = bf16[96,512]{1,0:T(8,128)(2,1)} copy(bf16[96,512]{1,0:T(8,128)(2,1)} %get-tuple-element.4) | data formatting | bytes 196608
  31.3 1.9 %copy.25 = bf16[512,512]{1,0:T(8,128)(2,1)} copy(bf16[512,512]{1,0:T(8,128)(2,1)} %get-tuple-element.5) | data formatting | bytes 1048576

commit v3 on v2

--- a/solution.py
+++ b/solution.py
@@ -148,7 +148,7 @@
         edge_acc[here, :] = mm(edges[here, :], pe_in[0:width, :])
         return carry
 
-    lax.fori_loop(0, n_edges // BLOCK, edge_first, 0)
+    lax.fori_loop(0, n_edges // BLOCK, edge_first, 0, unroll=True)
 
     got = list_dst.at[pl.ds(1, n - 1)]
     pltpu.make_async_copy(got, got, list_recv).wait()
@@ -194,7 +194,7 @@
         grid_acc[here, :] = mm(gedges[here, :], ge_in[0:width, :]) + mm(repeat, term)
         return carry
 
-    lax.fori_loop(0, n_gedges // BLOCK, grid_first, 0)
+    lax.fori_loop(0, n_gedges // BLOCK, grid_first, 0, unroll=True)
     load(9).wait()
     gnode_acc[...] = mm(glat[...], gn_in[0:width, :])
     for k in (4, 6, 15, 16, 17, 18, 19):
@@ -229,7 +229,7 @@
         incoming[...] += mm(pick(iota((rows, BLOCK), 0) == receivers), message)
         return carry
 
-    lax.fori_loop(0, n_edges // BLOCK, edge_second, 0)
+    lax.fori_loop(0, n_edges // BLOCK, edge_second, 0, unroll=True)
 
     node_sum = node_own + mm(incoming[...].astype(BF16), pn_in[width:, :])
     mesh_new = (
@@ -259,7 +259,7 @@
         grid_acc[here, :] += mm_t(gather, own_term[...])
         return carry
 
-    lax.fori_loop(0, n_gedges // BLOCK, grid_own, 0)
+    lax.fori_loop(0, n_gedges // BLOCK, grid_own, 0, unroll=True)
     side_copy(0).wait_recv()
     side_copy(1).wait_recv()
     pooled = pick(iota((nodes, BLOCK), 1) // NEAR == iota((nodes, BLOCK), 0))
@@ -276,7 +276,7 @@
         gin[there, :] = mm(pooled, message).astype(BF16)
         return carry
 
-    lax.fori_loop(0, n_gedges // BLOCK, grid_second, 0)
+    lax.fori_loop(0, n_gedges // BLOCK, grid_second, 0, unroll=True)
 
     def grid_node(b, carry):
         there = pl.ds(pl.multiple_of(b * (n_grid // 2), n_grid // 2), n_grid // 2)
@@ -285,7 +285,7 @@
         grid_out[there, :] = (glat[there, :].astype(F32) + update).astype(BF16)
         return carry
 
-    lax.fori_loop(0, 2, grid_node, 0)
+    lax.fori_loop(0, 2, grid_node, 0, unroll=True)
 
     sent = list_src.at[pl.ds(1, n - 1)]
     pltpu.make_async_copy(sent, sent, list_send).wait()
@@ -352,8 +352,8 @@
     return pl.pallas_call(
         functools.partial(kernel, n),
         out_shape=(
-            jax.ShapeDtypeStruct(mesh_latent.shape, BF16),
-            jax.ShapeDtypeStruct(grid_latent.shape, BF16),
+            pltpu.VMEM(mesh_latent.shape, BF16),
+            pltpu.VMEM(grid_latent.shape, BF16),
         ),
         in_specs=[pl.BlockSpec(memory_space=pltpu.HBM)] * len(big + small),
         out_specs=(vmem, vmem),

time: 33.3 us -> 28.7 us (0.86)
  Pallas kernels: 29.1 us -> 26.4 us
  local copies, waits for them, and re-layouts: 3.41 us -> 1.44 us
    pallas_call x1, Pallas kernels: 29.1 us -> 26.4 us  [local(): pl.pallas_call(functools.partial(kernel, n), out_shape=(pltpu.VMEM(mesh_l...]
    unnamed x2, local copies, waits for them, and re-layouts: 3.41 us -> 1.44 us
where the time goes in v3:
time: 28.7 us; the launch traced here: 28.5 us
  Pallas kernels  26.4 us (92%)
  local copies, waits for them, and re-layouts  1.44 us (5%)
  between operations  0.65 us (2%)
    pallas_call x1, Pallas kernels, local(): pl.pallas_call(functools.partial(kernel, n), out_shape=(pltpu.VMEM(mesh_l...  26.4 us
    unnamed x2, local copies, waits for them, and re-layouts  1.44 us

profile of v3, /device:TPU:1, one launch (start us, length us, event | category | flops | bytes accessed | tf_op | source)
XLA Modules:
  0.0 28.5 jit_solution(2222532914833828080)
XLA Ops:
  0.6 26.4 %shard_map.203 = (bf16[96,512]{1,0:T(8,128)(2,1)S(1)}, bf16[512,512]{1,0:T(8,128)(2,1)S(1)}) custom-call(bf16[1152,512]{1,0:T(8,128)(2,1)} %refs_0_.1, bf16[512,512]{1,0:T(8,128)(2,1)} %refs_1_.1, bf16[1536,512]{1,0:T(8,128)(2,1)} %refs_2_.1, bf16[1536,512]{1,0:T(8,128)(2,1)} %refs_3_.1, bf16[512,512]{1,0:T(8,128)(2,1)} %refs_4_.1, ...), custom_call_target="tpu_custom_call" | custom-call | tf_op jit(solution)/shard_map/pallas_call | solution.py:352
  27.0 0.6 %copy.24 = bf16[96,512]{1,0:T(8,128)(2,1)} copy(bf16[96,512]{1,0:T(8,128)(2,1)S(1)} %get-tuple-element.2) | data formatting | bytes 196608
  27.7 0.8 %copy.25 = bf16[512,512]{1,0:T(8,128)(2,1)} copy(bf16[512,512]{1,0:T(8,128)(2,1)S(1)} %get-tuple-element.3) | data formatting | bytes 1048576

commit v4 on v3

--- a/solution.py
+++ b/solution.py
@@ -104,7 +104,7 @@
         pl.semaphore_signal(barrier, inc=1, device_id={"lon": at(d)}, device_id_type=MESH_ID)
         return carry
 
-    lax.fori_loop(1, n, greet, 0)
+    lax.fori_loop(1, n, greet, 0, unroll=n <= 16)
 
     def spread_list(o, carry):
         kept = jnp.where(iota((cap, n), 1) == o, lists[...].astype(F32), 0.0)
@@ -130,7 +130,7 @@
         list_copy(d).start()
         return carry
 
-    lax.fori_loop(1, n, send_list, 0)
+    lax.fori_loop(1, n, send_list, 0, unroll=n <= 16)
     list_dst[0] = list_src[me]
 
     load(11).wait()
@@ -175,7 +175,7 @@
         rows_copy(d).start()
         return carry
 
-    lax.fori_loop(1, n, send_rows, 0)
+    lax.fori_loop(1, n, send_rows, 0, unroll=n <= 16)
     rows_dst[0:chunk, :] = rows_src[0:chunk, :]
 
     for k in (13, 14, 5, 7):

time: 28.7 us -> 28.6 us (level)
  no operation moved by 1% of the time
where the time goes in v4:
time: 28.6 us; the launch traced here: 28.4 us
  Pallas kernels  26.4 us (92%)
  local copies, waits for them, and re-layouts  1.44 us (5%)
  between operations  0.65 us (2%)
    pallas_call x1, Pallas kernels, local(): pl.pallas_call(functools.partial(kernel, n), out_shape=(pltpu.VMEM(mesh_l...  26.4 us
    unnamed x2, local copies, waits for them, and re-layouts  1.44 us

profile of v4, /device:TPU:1, one launch (start us, length us, event | category | flops | bytes accessed | tf_op | source)
XLA Modules:
  0.0 28.4 jit_solution(5065781110782059877)
XLA Ops:
  0.6 26.4 %shard_map.203 = (bf16[96,512]{1,0:T(8,128)(2,1)S(1)}, bf16[512,512]{1,0:T(8,128)(2,1)S(1)}) custom-call(bf16[1152,512]{1,0:T(8,128)(2,1)} %refs_0_.1, bf16[512,512]{1,0:T(8,128)(2,1)} %refs_1_.1, bf16[1536,512]{1,0:T(8,128)(2,1)} %refs_2_.1, bf16[1536,512]{1,0:T(8,128)(2,1)} %refs_3_.1, bf16[512,512]{1,0:T(8,128)(2,1)} %refs_4_.1, ...), custom_call_target="tpu_custom_call" | custom-call | tf_op jit(solution)/shard_map/pallas_call | solution.py:352
  27.0 0.6 %copy.24 = bf16[96,512]{1,0:T(8,128)(2,1)} copy(bf16[96,512]{1,0:T(8,128)(2,1)S(1)} %get-tuple-element.2) | data formatting | bytes 196608
  27.7 0.8 %copy.25 = bf16[512,512]{1,0:T(8,128)(2,1)} copy(bf16[512,512]{1,0:T(8,128)(2,1)S(1)} %get-tuple-element.3) | data formatting | bytes 1048576
